TPU v7x, 32 devices: a whole 2x2x4 slice. The times are simulated.
32 devices in a mesh: grp: 4 (over y, x), wide: 8 (over z, core).
Axes of the slice: x: 2, y: 2, z: 4, core: 2. Of those that a mesh axis runs over, the one named last changes fastest.
Arguments:
- tiles: bfloat16 [1536, 256, 256], P(('grp', 'wide')), may hold values from -0.59765625 to 0.59765625
- contraction: int32 [1536], P(('grp', 'wide')), may hold values from 0 to 15
- row_tile: int32 [1536], P(('grp', 'wide')), may hold values from 0 to 31, as said below
- owner_map: int32 [32], replicated, may hold values from 0 to 31, as said below
- panel: bfloat16 [4096, 768], P('grp'), may hold values from -0.5390625 to 0.5390625
Outputs:
- column_block: float32 [8192, 768], P('wide')
Inputs may be any that keep to these rules, and one draw needn't show every extreme that they name: `row_tile`: every row tile's owner is owner_map // 4; among the 48 contributions of one device at most 16 have row tiles of one owner, and on every device some owner gets exactly 16. `owner_map`: A permutation of the row tiles.
All inputs are finite; a program needn't handle non-finite values.
Results may differ from a plain program's by a relative error of at most 0.0003.
Values may be sent and summed in bfloat16 or wider, within the bound.
No kernel may reach another device: no remote copies, remote signals or barrier semaphores. Data moves between devices by JAX's collectives and lax.ppermute only.
A program may use at most 192 MiB of HBM per device.

v0:
```python
import math

import jax
import jax.numpy as jnp
from jax import lax
from jax.sharding import PartitionSpec as P


def place_slots(row_ids, owner_map, out_dev):
    table_ids = jnp.arange(owner_map.shape[0], dtype=jnp.int32)
    position = jnp.sum(jnp.where(row_ids[..., None] == table_ids, owner_map, 0), axis=-1)
    target = position // out_dev
    serial = jnp.arange(row_ids.shape[-1], dtype=jnp.int32)
    earlier = (target[..., :, None] == target[..., None, :]) & (serial[:, None] > serial[None, :])
    ranking = jnp.sum(earlier.astype(jnp.int32), axis=-1)
    return (position % out_dev, target, ranking)


def add_products(summed, arrived, slot_labels, panel_tiles):
    slot_count = arrived.shape[0]
    block_rows = math.gcd(slot_count, 32)
    out_dev = summed.shape[0]
    local_ids = jnp.arange(out_dev, dtype=jnp.int32)

    def one_block(which_block, running, source_tiles, source_labels):
        part_tiles = lax.dynamic_slice_in_dim(source_tiles, which_block * block_rows, block_rows, 0)
        part_labels = lax.dynamic_slice_in_dim(
            source_labels, which_block * block_rows, block_rows, 0
        )
        chosen = jnp.take(panel_tiles, part_labels[:, 1], axis=0)
        products = jnp.einsum(
            "sab,sbc->sac", part_tiles, chosen, preferred_element_type=jnp.float32
        )
        row_hits = (part_labels[:, 0][:, None] == local_ids[None, :]).astype(jnp.float32)
        return running + jnp.einsum(
            "sr,sac->rac", row_hits, products, precision=lax.Precision.HIGHEST
        )

    return lax.fori_loop(
        0,
        slot_count // block_rows,
        lambda which_block, running: one_block(which_block, running, arrived, slot_labels),
        summed,
    )


def per_device(tiles, contraction, row_tile, owner_map, panel):
    wide_count = lax.axis_size("wide")
    tile_dev = tiles.shape[0]
    tile_side = tiles.shape[1]
    out_dev = owner_map.shape[0] // wide_count
    most_slots = tile_dev * 8 // (3 * wide_count)
    slot_total = wide_count * most_slots
    local_row, target, ranking = place_slots(row_tile, owner_map, out_dev)
    slot_index = target * most_slots + ranking
    outgoing = jnp.zeros((slot_total, tile_side, tile_side), tiles.dtype).at[slot_index].set(tiles)
    all_rows, all_contraction = (
        lax.all_gather(row_tile, "wide", axis=0, tiled=True),
        lax.all_gather(contraction, "wide", axis=0, tiled=True),
    )
    all_rows = all_rows.reshape(wide_count, tile_dev)
    all_contraction = all_contraction.reshape(wide_count, tile_dev)
    source_local, source_target, source_rank = place_slots(all_rows, owner_map, out_dev)
    source_ids = jnp.arange(wide_count, dtype=jnp.int32)
    mine = source_target == lax.axis_index("wide")
    arrive_index = jnp.where(mine, source_ids[:, None] * most_slots + source_rank, slot_total)
    label_pairs = jnp.stack([source_local, all_contraction], axis=-1).reshape(
        wide_count * tile_dev, 2
    )
    vacant_label = jnp.stack(
        [jnp.full((slot_total,), out_dev, jnp.int32), jnp.zeros((slot_total,), jnp.int32)], axis=1
    )
    arrived_labels = vacant_label.at[arrive_index.reshape(-1)].set(label_pairs, mode="drop")
    gathered = lax.all_gather(panel, "grp", axis=0, tiled=True)
    panel_tiles = gathered.reshape(gathered.shape[0] // tile_side, tile_side, gathered.shape[1])
    summed = jnp.zeros((out_dev, tile_side, gathered.shape[1]), jnp.float32)
    arrived = lax.all_to_all(outgoing, "wide", split_axis=0, concat_axis=0, tiled=True)
    summed = add_products(summed, arrived, arrived_labels, panel_tiles)
    summed = lax.psum(summed, "grp")
    return summed.reshape(out_dev * tile_side, gathered.shape[1])


def solution(mesh):
    return jax.shard_map(
        per_device,
        mesh=mesh,
        in_specs=(
            P(("grp", "wide"), None, None),
            P(("grp", "wide")),
            P(("grp", "wide")),
            P(),
            P("grp", None),
        ),
        out_specs=P("wide", None),
        check_vma=False,
    )
```

profile of v0, /device:TPU:0, one launch (start us, length us, event | category | flops | bytes accessed | tf_op | source)
XLA Modules:
  0.0 734.9 jit_solution(9783212228602511749)
XLA Ops:
  6.5 0.8 select_reduce_fusion.1
  7.5 5.9 broadcast_in_dim.68
  13.4 16.8 %scatter_fusion.1 = bf16[128,256,256]{2,1,0:T(8,128)(2,1)} fusion(bf16[128,256,256]{2,1,0:T(8,128)(2,1)} %broadcast_in_dim.68, s32[48]{0:T(128)S(1)} %fusion.20, bf16[48,256,256]{2,1,0:T(8,128)(2,1)} %param.7), kind=kCustom, calls=%fused_computation.2 | custom fusion | bytes 18874560 | tf_op jit(solution)/shard_map/scatter | solution.py:56
  30.2 6.5 all-to-all-start
  36.8 0.7 all-gather.2.cloned.1.call-update
  37.6 0.6 dynamic-slice
  39.2 361.7 %all-reduce.2 = (s32[384]{0:T(512)S(1)}, s32[384]{0:T(512)S(1)}) all-reduce(s32[384]{0:T(512)S(1)} %dynamic-update-slice, s32[384]{0:T(512)S(1)} %dynamic-update-slice.1), channel_id=1, replica_groups=mesh['grp'=4,'wide'=8] {'wide'}, use_global_device_ids=true, to_apply=%add | all-reduce | flops 768 | bytes 6144
  401.9 1.5 scatter_fusion
  403.5 231.9 %while.14 = (s32[]{:T(128)}, f32[4,256,768]{2,0,1:T(4,128)S(1)}, s32[128,2]{0,1:T(2,128)S(1)}, bf16[128,256,256]{2,1,0:T(8,128)(2,1)}, bf16[16,256,768]{2,1,0:T(...) while((s32[]{:T(128)}, f32[4,256,768]{2,0,1:T(4,128)S(1)}, ...), condition=%wide.region_7.8_spmd.clone, body=%wide.region_6.7_spmd.clone.sunk | while | flops 3531081216 | bytes 98572000 | solution.py:39
  403.8 9.3 %gather_fusion = bf16[32,256,768]{2,1,0:T(8,128)(2,1)} fusion(bf16[16,256,768]{2,1,0:T(8,128)(2,1)} %get-tuple-element.223, s32[1024]{0:T(1024)S(1)} %pad_clamp_fusion.2), kind=kCustom, calls=%fused_computation.clone.clone.1 | custom fusion | bytes 25165952 | tf_op jit(solution)/shard_map/while/body/eval_jaxpr/jit(_take)/gather | solution.py:30
  413.1 17.7 %fusion.30 = f32[32,256,768]{2,1,0:T(8,128)} fusion(bf16[32,256,768]{2,1,0:T(8,128)(2,1)} %gather_fusion, pred[32]{0:T(512)(128)(4,1)S(1)} %and_bitcast_fusion.2, bf16[128,256,256]{2,1,0:T(8,128)(2,1)} %get-tuple-element.222, s32[]{:T(128)S(6)} %select_n.173), kind=kOutput, calls=%fused_computation.6.clone.1 | convolution fusion | flops 3227516928 | bytes 41943076 | tf_op jit(solution)/shard_map/while/body/eval_jaxpr/sab,sbc->sac/dot_general | solution.py:31
  430.8 30.7 %select_add_fusion.2 = f32[4,256,768]{2,0,1:T(4,128)S(1)} fusion(f32[4,256,768]{2,0,1:T(4,128)S(1)} %get-tuple-element.211, pred[]{:T(512)S(6)} %compare.49, f32[32,256,768]{2,1,0:T(8,128)} %fusion.30, s32[32]{0:T(128)S(1)} %get-tuple-element.200), kind=kOutput, calls=%fused_computation.11.clone.1 | convolution fusion | flops 303562880 | bytes 31457408 | tf_op jit(solution)/shard_map/while/body/eval_jaxpr/sr,sac->rac/dot_general | solution.py:35
  461.6 9.5 %gather_fusion = bf16[32,256,768]{2,1,0:T(8,128)(2,1)} fusion(bf16[16,256,768]{2,1,0:T(8,128)(2,1)} %get-tuple-element.223, s32[1024]{0:T(1024)S(1)} %pad_clamp_fusion.2), kind=kCustom, calls=%fused_computation.clone.clone.1 | custom fusion | bytes 25165952 | tf_op jit(solution)/shard_map/while/body/eval_jaxpr/jit(_take)/gather | solution.py:30
  471.2 17.7 %fusion.30 = f32[32,256,768]{2,1,0:T(8,128)} fusion(bf16[32,256,768]{2,1,0:T(8,128)(2,1)} %gather_fusion, pred[32]{0:T(512)(128)(4,1)S(1)} %and_bitcast_fusion.2, bf16[128,256,256]{2,1,0:T(8,128)(2,1)} %get-tuple-element.222, s32[]{:T(128)S(6)} %select_n.173), kind=kOutput, calls=%fused_computation.6.clone.1 | convolution fusion | flops 3227516928 | bytes 41943076 | tf_op jit(solution)/shard_map/while/body/eval_jaxpr/sab,sbc->sac/dot_general | solution.py:31
  488.8 30.7 %select_add_fusion.2 = f32[4,256,768]{2,0,1:T(4,128)S(1)} fusion(f32[4,256,768]{2,0,1:T(4,128)S(1)} %get-tuple-element.211, pred[]{:T(512)S(6)} %compare.49, f32[32,256,768]{2,1,0:T(8,128)} %fusion.30, s32[32]{0:T(128)S(1)} %get-tuple-element.200), kind=kOutput, calls=%fused_computation.11.clone.1 | convolution fusion | flops 303562880 | bytes 31457408 | tf_op jit(solution)/shard_map/while/body/eval_jaxpr/sr,sac->rac/dot_general | solution.py:35
  519.7 9.3 %gather_fusion = bf16[32,256,768]{2,1,0:T(8,128)(2,1)} fusion(bf16[16,256,768]{2,1,0:T(8,128)(2,1)} %get-tuple-element.223, s32[1024]{0:T(1024)S(1)} %pad_clamp_fusion.2), kind=kCustom, calls=%fused_computation.clone.clone.1 | custom fusion | bytes 25165952 | tf_op jit(solution)/shard_map/while/body/eval_jaxpr/jit(_take)/gather | solution.py:30
  529.0 17.7 %fusion.30 = f32[32,256,768]{2,1,0:T(8,128)} fusion(bf16[32,256,768]{2,1,0:T(8,128)(2,1)} %gather_fusion, pred[32]{0:T(512)(128)(4,1)S(1)} %and_bitcast_fusion.2, bf16[128,256,256]{2,1,0:T(8,128)(2,1)} %get-tuple-element.222, s32[]{:T(128)S(6)} %select_n.173), kind=kOutput, calls=%fused_computation.6.clone.1 | convolution fusion | flops 3227516928 | bytes 41943076 | tf_op jit(solution)/shard_map/while/body/eval_jaxpr/sab,sbc->sac/dot_general | solution.py:31
  546.7 30.7 %select_add_fusion.2 = f32[4,256,768]{2,0,1:T(4,128)S(1)} fusion(f32[4,256,768]{2,0,1:T(4,128)S(1)} %get-tuple-element.211, pred[]{:T(512)S(6)} %compare.49, f32[32,256,768]{2,1,0:T(8,128)} %fusion.30, s32[32]{0:T(128)S(1)} %get-tuple-element.200), kind=kOutput, calls=%fused_computation.11.clone.1 | convolution fusion | flops 303562880 | bytes 31457408 | tf_op jit(solution)/shard_map/while/body/eval_jaxpr/sr,sac->rac/dot_general | solution.py:35
  577.6 9.4 %gather_fusion = bf16[32,256,768]{2,1,0:T(8,128)(2,1)} fusion(bf16[16,256,768]{2,1,0:T(8,128)(2,1)} %get-tuple-element.223, s32[1024]{0:T(1024)S(1)} %pad_clamp_fusion.2), kind=kCustom, calls=%fused_computation.clone.clone.1 | custom fusion | bytes 25165952 | tf_op jit(solution)/shard_map/while/body/eval_jaxpr/jit(_take)/gather | solution.py:30
  587.0 17.7 %fusion.30 = f32[32,256,768]{2,1,0:T(8,128)} fusion(bf16[32,256,768]{2,1,0:T(8,128)(2,1)} %gather_fusion, pred[32]{0:T(512)(128)(4,1)S(1)} %and_bitcast_fusion.2, bf16[128,256,256]{2,1,0:T(8,128)(2,1)} %get-tuple-element.222, s32[]{:T(128)S(6)} %select_n.173), kind=kOutput, calls=%fused_computation.6.clone.1 | convolution fusion | flops 3227516928 | bytes 41943076 | tf_op jit(solution)/shard_map/while/body/eval_jaxpr/sab,sbc->sac/dot_general | solution.py:31
  604.6 30.7 %select_add_fusion.2 = f32[4,256,768]{2,0,1:T(4,128)S(1)} fusion(f32[4,256,768]{2,0,1:T(4,128)S(1)} %get-tuple-element.211, pred[]{:T(512)S(6)} %compare.49, f32[32,256,768]{2,1,0:T(8,128)} %fusion.30, s32[32]{0:T(128)S(1)} %get-tuple-element.200), kind=kOutput, calls=%fused_computation.11.clone.1 | convolution fusion | flops 303562880 | bytes 31457408 | tf_op jit(solution)/shard_map/while/body/eval_jaxpr/sr,sac->rac/dot_general | solution.py:35
  635.4 2.2 copy.16
  637.7 86.7 %all-reduce.5.cloned.1.call-done = f32[1024,768]{1,0:T(8,128)} async-done(((f32[1024,768]{1,0:T(8,128)}), f32[1024,768]{1,0:T(8,128)}) %all-reduce.5.cloned.1.call-update) | async-done | bytes 3145744 | tf_op jit(solution)/shard_map/psum | solution.py:79
  724.3 3.8 copy.38
  (53 shorter events, 2.2 us)
Async XLA Ops:
  30.2 7.4 %copy-start.4 = (u32[32]{0:T(128)S(1)}, u32[32]{0:T(128)}, u32[]{:S(2)}) copy-start(u32[32]{0:T(128)} %constant.119) | copy-start | bytes 388
  30.2 8.5 %copy-start.2 = (s32[48]{0:T(128)S(1)}, s32[48]{0:T(128)}, u32[]{:S(2)}) copy-start(s32[48]{0:T(128)} %param.9) | copy-start | bytes 580
  30.2 8.8 %copy-start.3 = (s32[48]{0:T(128)S(1)}, s32[48]{0:T(128)}, u32[]{:S(2)}) copy-start(s32[48]{0:T(128)} %param.8) | copy-start | bytes 580
  30.2 370.8 %copy-start.1 = (s32[32]{0:T(128)S(1)}, s32[32]{0:T(128)}, u32[]{:S(2)}) copy-start(s32[32]{0:T(128)} %param.10) | copy-start | bytes 388
  30.2 371.7 %copy-start = (s32[128,2]{1,0:T(8,128)S(1)}, s32[128,2]{1,0:T(8,128)}, u32[]{:S(2)}) copy-start(s32[128,2]{1,0:T(8,128)} %constant.111.clone.1) | copy-start | bytes 3076
  30.2 373.2 %all-to-all-start = ((bf16[128,256,256]{2,1,0:T(8,128)(2,1)}), bf16[128,256,256]{2,1,0:T(8,128)(2,1)}, u32[]{:S(2)}, u32[]{:S(2)}) async-start(bf16[128,256,256]{2,1,0:T(8,128)(2,1)} %scatter_fusion.1), calls=%async_computation | async-start | bytes 33554432 | tf_op jit(solution)/shard_map/all_to_all | solution.py:77
  36.8 366.7 %all-gather.2.cloned.1.call-start = ((), (), s32[]{:S(2)}) async-start(), calls=%async_computation.1 | async-start | bytes 7864320 | tf_op jit(solution)/shard_map/all_gather | solution.py:74
  37.5 686.8 %all-reduce.5.cloned.1.call-start = ((), (), s32[]{:S(2)}) async-start(), calls=%async_computation.2 | async-start | bytes 6291456 | tf_op jit(solution)/shard_map/psum | solution.py:79
Sparse Core Ops, SparseCore 0:
  39.5 72.3 all-gather.1
  637.8 86.5 all-reduce.4
where the time goes:
time: 735 us
  blocking collectives  362 us (49%)
  matrix products  194 us (26%)
  waiting for transfers between devices  87.4 us (12%)
  local copies, waits for them, and re-layouts  69.5 us (9%)
  between operations  14.1 us (2%)
    unnamed x1, blocking collectives  362 us
    dot_general x4, matrix products, one_block(): jnp.einsum('sr,sac->rac', row_hits, products, precision=lax.Precision.HIG...  123 us
    psum x1, waiting for transfers between devices, per_device(): summed = lax.psum(summed, 'grp')  86.7 us
    dot_general x4, matrix products, one_block(): jnp.einsum('sab,sbc->sac', part_tiles, chosen, preferred_element_type=jnp...  70.7 us
    gather x4, local copies, waits for them, and re-layouts, one_block(): chosen = jnp.take(panel_tiles, part_labels[:, 1], axis=0)  37.5 us
    scatter x1, local copies, waits for them, and re-layouts, per_device(): jnp.zeros((slot_total, tile_side, tile_side), tiles.dtype).at[slot_index]  16.8 us
  transfers between devices with their start and end apart: 3, of which 1 were waited for; matrix products, arithmetic and copies ran while one was open for 0% of the time, Pallas kernels for 0%

commit v1 on v0

--- a/solution.py
+++ b/solution.py
@@ -1,9 +1,20 @@
+import functools
 import math
 
 import jax
 import jax.numpy as jnp
 from jax import lax
+from jax.experimental import pallas as pl
+from jax.experimental.pallas import tpu as pltpu
 from jax.sharding import PartitionSpec as P
+
+MIB = 1024 * 1024
+CODE_ROWS = 16
+CODE_STEPS = 256.0
+TOP = 32000.0
+CHUNK = 256
+UNROLL = 4
+LOG2 = math.log(2.0)
 
 
 def place_slots(row_ids, owner_map, out_dev):
@@ -44,7 +55,7 @@
     )
 
 
-def per_device(tiles, contraction, row_tile, owner_map, panel):
+def slots_plan(tiles, contraction, row_tile, owner_map, panel):
     wide_count = lax.axis_size("wide")
     tile_dev = tiles.shape[0]
     tile_side = tiles.shape[1]
@@ -78,6 +89,302 @@
     summed = add_products(summed, arrived, arrived_labels, panel_tiles)
     summed = lax.psum(summed, "grp")
     return summed.reshape(out_dev * tile_side, gathered.shape[1])
+
+
+def encode(value):
+    largest = jnp.max(jnp.abs(value), axis=0, keepdims=True)
+    code = jnp.ceil(jnp.log(jnp.maximum(largest, 1e-30)) * (CODE_STEPS / LOG2))
+    scale = jnp.exp(code * (-LOG2 / CODE_STEPS)) * TOP
+    whole = jnp.round(value * scale).astype(jnp.int32).astype(jnp.int16)
+    return whole, code.astype(jnp.int32)
+
+
+def put_encoded(ref, value):
+    side = value.shape[0]
+    whole, code = encode(value)
+    ref[pl.ds(0, side), :] = whole
+    ref[pl.ds(side, CODE_ROWS), :] = jnp.broadcast_to(
+        code, (CODE_ROWS, code.shape[1])
+    ).astype(jnp.int16)
+
+
+def get_decoded(ref, side):
+    code = ref[pl.ds(side, CODE_ROWS), :].astype(jnp.int32).astype(jnp.float32)[:1]
+    scale = jnp.exp(code * (LOG2 / CODE_STEPS)) * (1.0 / TOP)
+    return ref[pl.ds(0, side), :].astype(jnp.int32).astype(jnp.float32) * scale
+
+
+def products_kernel(
+    pieces, ends_ref, source_ref, slot_ref, label_ref,
+    own_tiles, sib_tiles, own_panel, d1, d2, d3, s1, s2, s3,
+    send, keep, held, stack, acc, sems,
+):
+    tile_dev, side = held.shape[1], held.shape[2]
+    shard = own_panel.shape[0] // side
+    half = shard // 2
+    outs = send.shape[0]
+    copies = []
+    for q, (which, first, count) in enumerate(pieces):
+        tiles = (own_tiles, sib_tiles)[which]
+        copies.append(
+            pltpu.make_async_copy(
+                tiles.at[pl.ds(first, count)], held.at[which, pl.ds(first, count)], sems.at[q]
+            )
+        )
+        copies[-1].start()
+    for t in range(shard):
+        stack[t] = own_panel[pl.ds(t * side, side), :]
+    for d, (near, far) in enumerate(((d1, s1), (d2, s2), (d3, s3)), 1):
+        for t in range(half):
+            stack[d * shard + t] = near[pl.ds(t * side, side), :]
+            stack[d * shard + half + t] = far[pl.ds(t * side, side), :]
+
+    @pl.loop(0, acc.shape[0])
+    def _(i):
+        acc[i] = jnp.zeros(acc.shape[1:], jnp.float32)
+
+    def some(which, at, count):
+        found = [
+            jnp.dot(
+                held[which, source_ref[which, at + u]],
+                stack[label_ref[which, at + u]],
+                preferred_element_type=jnp.float32,
+            )
+            for u in range(count)
+        ]
+        for u in range(count):
+            acc[slot_ref[which, at + u]] += found[u]
+
+    for q, (which, first, count) in enumerate(pieces):
+        copies[q].wait()
+        begin = 0 if first == 0 else ends_ref[q - 1]
+        end = ends_ref[q]
+        rounds = (end - begin) // UNROLL
+
+        @pl.loop(0, rounds)
+        def _(i, which=which, begin=begin):
+            some(which, begin + i * UNROLL, UNROLL)
+
+        @pl.loop(begin + rounds * UNROLL, end)
+        def _(i, which=which):
+            some(which, i, 1)
+
+    @pl.loop(0, outs)
+    def _(i):
+        put_encoded(send.at[i], acc[i])
+
+    @pl.loop(0, outs)
+    def _(i):
+        keep[i] = acc[outs + i]
+
+
+def stage_kernel(low, bit_ref, recv, kept, send, keep):
+    side = kept.shape[1]
+    bit = bit_ref[0]
+
+    @pl.loop(0, send.shape[0])
+    def _(i):
+        base = (i // low) * (2 * low) + i % low
+        other, mine = base + (1 - bit) * low, base + bit * low
+        put_encoded(send.at[i], kept[other] + get_decoded(recv.at[other], side))
+        keep[i] = kept[mine] + get_decoded(recv.at[mine], side)
+
+
+def finish_kernel(recv, kept, out):
+    put_encoded(out, kept[0] + get_decoded(recv.at[0], kept.shape[1]))
+
+
+def spread_kernel(*refs):
+    blocks, out = refs[0], refs[-1]
+    side = blocks.shape[1] - CODE_ROWS
+    for i in range(blocks.shape[0]):
+        out[pl.ds(i * side, side), :] = get_decoded(blocks.at[i], side)
+
+
+def in_vmem(count):
+    return [pl.BlockSpec(memory_space=pltpu.VMEM)] * count
+
+
+def in_smem(count):
+    return [pl.BlockSpec(memory_space=pltpu.SMEM)] * count
+
+
+def in_any(count):
+    return [pl.BlockSpec(memory_space=pl.ANY)] * count
+
+
+def shape(dims, kind):
+    return jax.ShapeDtypeStruct(dims, kind)
+
+
+def params(mib):
+    return pltpu.CompilerParams(vmem_limit_bytes=mib * MIB)
+
+
+def cost(flops, moved):
+    return pl.CostEstimate(flops=flops, bytes_accessed=moved, transcendentals=0)
+
+
+def compact(match, values):
+    count = match.shape[-1]
+    rank = jnp.cumsum(match.astype(jnp.int32), axis=-1) - 1
+    at = jnp.arange(count, dtype=jnp.int32)
+    hit = match[:, None, :] & (rank[:, None, :] == at[None, :, None])
+    return [jnp.sum(jnp.where(hit, v[:, None, :], 0), axis=-1) for v in values]
+
+
+def sums_plan(tiles, contraction, row_tile, owner_map, panel):
+    wide_count = lax.axis_size("wide")
+    tile_dev, side = tiles.shape[0], tiles.shape[1]
+    out_dev = owner_map.shape[0] // wide_count
+    rows, columns = panel.shape
+    shard = rows // side
+    chunks = columns // CHUNK
+    sums = owner_map.shape[0] // 2
+    g, w = lax.axis_index("grp"), lax.axis_index("wide")
+    core = w % 2
+
+    def to_core(v):
+        return lax.ppermute(v, "wide", [(i, i ^ 1) for i in range(wide_count)])
+
+    def to_grp(v, d):
+        return lax.ppermute(v, "grp", [(i, i ^ d) for i in range(4)])
+
+    dims = {
+        "x": (0, g % 2, lambda v: to_grp(v, 1)),
+        "y": (1, g // 2, lambda v: to_grp(v, 2)),
+    }
+    for b in range((wide_count // 2).bit_length() - 1):
+        pairs = [(i, i ^ (2 << b)) for i in range(wide_count)]
+        dims["z%d" % b] = (
+            2 + b,
+            (w // (2 << b)) % 2,
+            lambda v, pairs=pairs: lax.ppermute(v, "wide", pairs),
+        )
+    rest = [name for name in dims if name not in ("x", "y", "z0")]
+    orders = [["x", "y", "z0"] + rest, ["y", "x", "z0"] + rest, ["z0", "y", "x"] + rest]
+
+    labels = jnp.stack([row_tile, contraction])
+    both = jnp.stack([labels, to_core(labels)])
+    sib_tiles = to_core(tiles)
+
+    near, far = [], []
+    for j in range(chunks):
+        mine = lax.dynamic_slice(panel, (core * (rows // 2), j * CHUNK), (rows // 2, CHUNK))
+        if j > 0:
+            mine, *near[j - 1] = lax.optimization_barrier((mine, *near[j - 1]))
+        near.append([to_grp(mine, d) for d in (1, 2, 3)])
+    for j in range(chunks):
+        far.append([to_core(v) for v in near[j]])
+
+    table_ids = jnp.arange(owner_map.shape[0], dtype=jnp.int32)
+    position = jnp.sum(jnp.where(both[:, 0, :, None] == table_ids, owner_map, 0), axis=-1)
+    owner, local = position // out_dev, position % out_dev
+    index = (owner // 2) * out_dev + local
+    k = both[:, 1]
+    apart, inner = (k // shard) ^ g, k % shard
+    half = shard // 2
+    crossed = jnp.where(inner // half == core, 0, half) + inner % half
+    label = jnp.where(apart == 0, inner, apart * shard + crossed)
+    match = owner % 2 == core
+    serial = jnp.broadcast_to(jnp.arange(tile_dev, dtype=jnp.int32), match.shape)
+    source, index, label = compact(match, [serial, index, label])
+    cut = tile_dev // 4
+    pieces = ((0, 0, cut), (0, cut, tile_dev - cut), (1, 0, tile_dev))
+    ends = jnp.stack(
+        [
+            jnp.sum((match[which] & (serial[which] < first + count)).astype(jnp.int32))
+            for which, first, count in pieces
+        ]
+    )
+
+    result = None
+    for j in range(chunks):
+        order = orders[j % len(orders)]
+        left = ["z%d" % b for b in reversed(range(len(dims) - 2))] + ["y", "x"]
+        bit, own_bit, move = dims[order[0]]
+        low = 1 << bit
+        kept_here = (index // low) % 2 == own_bit
+        slot = (index // (2 * low)) * low + index % low + jnp.where(kept_here, sums // 2, 0)
+        left.remove(order[0])
+        send, keep = pl.pallas_call(
+            functools.partial(products_kernel, pieces),
+            grid=(1,),
+            in_specs=in_smem(4)
+            + in_any(2)
+            + [pl.BlockSpec((rows, CHUNK), lambda i, j=j: (0, j))]
+            + in_vmem(6),
+            out_specs=in_vmem(2),
+            out_shape=[
+                shape((sums // 2, side + CODE_ROWS, CHUNK), jnp.int16),
+                shape((sums // 2, side, CHUNK), jnp.float32),
+            ],
+            scratch_shapes=[
+                pltpu.VMEM((2, tile_dev, side, side), tiles.dtype),
+                pltpu.VMEM((4 * shard, side, CHUNK), panel.dtype),
+                pltpu.VMEM((sums, side, CHUNK), jnp.float32),
+                pltpu.SemaphoreType.DMA((len(pieces),)),
+            ],
+            compiler_params=params(40),
+            cost_estimate=cost(
+                2 * tile_dev * side * side * CHUNK, 4 * tile_dev * side * side
+            ),
+            name="products",
+        )(ends, source, slot, label, tiles, sib_tiles, panel, *near[j], *far[j])
+
+        for name in order[1:]:
+            recv = move(send)
+            _, own_bit, move = dims[name]
+            low = 1 << (len(left) - 1 - left.index(name))
+            left.remove(name)
+            count = keep.shape[0] // 2
+            send, keep = pl.pallas_call(
+                functools.partial(stage_kernel, low),
+                in_specs=in_smem(1) + in_vmem(2),
+                out_specs=in_vmem(2),
+                out_shape=[
+                    shape((count, side + CODE_ROWS, CHUNK), jnp.int16),
+                    shape((count, side, CHUNK), jnp.float32),
+                ],
+                compiler_params=params(16),
+                cost_estimate=cost(20 * count * side * CHUNK, 18 * count * side * CHUNK),
+                name="stage",
+            )(own_bit.astype(jnp.int32)[None], recv, keep)
+
+        done = pl.pallas_call(
+            finish_kernel,
+            in_specs=in_vmem(2),
+            out_specs=pl.BlockSpec(memory_space=pltpu.VMEM),
+            out_shape=shape((side + CODE_ROWS, CHUNK), jnp.int16),
+            compiler_params=params(16),
+            cost_estimate=cost(20 * side * CHUNK, 8 * side * CHUNK),
+            name="finish",
+        )(move(send), keep)
+
+        blocks = lax.all_gather(done, "grp", axis=0)
+        earlier = [] if result is None else [result]
+        result = pl.pallas_call(
+            spread_kernel,
+            grid=(1,),
+            in_specs=in_vmem(1) + in_any(len(earlier)),
+            out_specs=pl.BlockSpec((out_dev * side, CHUNK), lambda i, j=j: (0, j)),
+            out_shape=shape((out_dev * side, columns), jnp.float32),
+            input_output_aliases={1: 0} if earlier else {},
+            compiler_params=params(16),
+            cost_estimate=cost(4 * out_dev * side * CHUNK, 6 * out_dev * side * CHUNK),
+            name="spread",
+        )(blocks, *earlier)
+    return result
+
+
+def per_device(tiles, contraction, row_tile, owner_map, panel):
+    dense = owner_map.shape[0] <= tiles.shape[0]
+    wide_count = lax.axis_size("wide")
+    fits = lax.axis_size("grp") == 4 and wide_count >= 4 and wide_count & (wide_count - 1) == 0
+    out_dev = owner_map.shape[0] // wide_count
+    if dense and fits and out_dev == 4 and panel.shape[1] % CHUNK == 0:
+        return sums_plan(tiles, contraction, row_tile, owner_map, panel)
+    return slots_plan(tiles, contraction, row_tile, owner_map, panel)
 
 
 def solution(mesh):

time: 735 us -> 170 us (0.23)
  blocking collectives: 362 us -> 32 us
  matrix products: 194 us -> 0 us
  local copies, waits for them, and re-layouts: 69.5 us -> 4.7 us
  starting transfers between devices: 6.61 us -> 43.4 us
  waiting for transfers between devices: 87.4 us -> 58.6 us
  Pallas kernels: 0 us -> 27.1 us
  between operations: 14.1 us -> 0.26 us
    unnamed x1 -> x0, blocking collectives: 362 us -> none
    dot_general x8 -> x0, matrix products: 194 us -> none  [the longest x4 123 us: one_block(): jnp.einsum('sr,sac->rac', row_hits, products, precision=lax.Precision.HIG...]
    psum x1 -> x0, waiting for transfers between devices: 86.7 us -> none  [per_device(): summed = lax.psum(summed, 'grp')]
    ppermute x0 -> x32, waiting for transfers between devices: none -> 58.6 us  [the longest x15 39.5 us: to_grp(): return lax.ppermute(v, 'grp', [(i, i ^ d) for i in range(4)])]
    ppermute x0 -> x32, starting transfers between devices: none -> 43.4 us  [the longest x15 29.1 us: to_grp(): return lax.ppermute(v, 'grp', [(i, i ^ d) for i in range(4)])]
    gather x4 -> x0, local copies, waits for them, and re-layouts: 37.5 us -> none  [one_block(): chosen = jnp.take(panel_tiles, part_labels[:, 1], axis=0)]
    all_gather x0 -> x3, blocking collectives: none -> 32 us  [sums_plan(): blocks = lax.all_gather(done, 'grp', axis=0)]
    pallas_call x0 -> x18, Pallas kernels: none -> 27.1 us  [the longest x3 20.4 us: sums_plan(): pl.pallas_call(functools.partial(products_kernel, pieces), grid=(1,), in_...]
  transfers between devices with their start and end apart: 3 -> 32, of which waited for: 1 -> 14; matrix products, arithmetic and copies ran while one was open for 0% -> 4% of each run, Pallas kernels for 0% -> 14%
where the time goes in v1:
time: 170 us; the launch traced here: 171 us
  waiting for transfers between devices  58.6 us (34%)
  starting transfers between devices  43.4 us (26%)
  blocking collectives  32 us (19%)
  Pallas kernels  27.1 us (16%)
  local copies, waits for them, and re-layouts  4.7 us (3%)
  other arithmetic  4.49 us (3%)
    ppermute x15, waiting for transfers between devices, to_grp(): return lax.ppermute(v, 'grp', [(i, i ^ d) for i in range(4)])  39.5 us
    all_gather x3, blocking collectives, sums_plan(): blocks = lax.all_gather(done, 'grp', axis=0)  32 us
    ppermute x15, starting transfers between devices, to_grp(): return lax.ppermute(v, 'grp', [(i, i ^ d) for i in range(4)])  29.1 us
    pallas_call x3, Pallas kernels, sums_plan(): pl.pallas_call(functools.partial(products_kernel, pieces), grid=(1,), in_...  20.4 us
    ppermute x6, waiting for transfers between devices, sums_plan(): lax.ppermute(v, 'wide', pairs)  16 us
    ppermute x6, starting transfers between devices, sums_plan(): lax.ppermute(v, 'wide', pairs)  12.1 us
  transfers between devices with their start and end apart: 32, of which 14 were waited for; matrix products, arithmetic and copies ran while one was open for 4% of the time, Pallas kernels for 14%

profile of v1, /device:TPU:0, one launch (start us, length us, event | category | flops | bytes accessed | tf_op | source)
XLA Modules:
  0.0 170.6 jit_solution(5891647612095973184)
XLA Ops:
  2.4 2.6 %collective-permute-start.2 = (bf16[512,256]{1,0:T(8,128)(2,1)S(1)}, bf16[512,256]{1,0:T(8,128)(2,1)S(1)}, u32[]{:S(2)}, u32[]{:S(2)}) collective-permute-start(bf16[512,256]{1,0:T(8,128)(2,1)S(1)} %get-tuple-element.79), channel_id=1, source_target_pairs={{0,8},{8,0},{16,24},{24,16},{1,9},{9,1},{17,25},{25,17},{2,10},{10... | collective-permute-start | bytes 786440 | tf_op jit(solution)/shard_map/ppermute | solution.py:251
  7.2 3.0 %collective-permute-done = s32[2,48]{1,0:T(2,128)S(1)} collective-permute-done((s32[2,48]{1,0:T(2,128)S(1)}, s32[2,48]{1,0:T(2,128)S(1)}, u32[]{:S(2)}, u32[]{:S(2)}) %collective-permute-start) | collective-permute-done | bytes 416 | tf_op jit(solution)/shard_map/ppermute | solution.py:248
  12.1 6.8 %collective-permute-done.3.d2 = bf16[512,256]{1,0:T(8,128)(2,1)S(1)} collective-permute-done((bf16[512,256]{1,0:T(8,128)(2,1)S(1)}, bf16[512,256]{1,0:T(8,128)(2,1)S(1)}, u32[]{:S(2)}, u32[]{:S(2)}) %collective-permute-start.3) | collective-permute-done | bytes 262176 | tf_op jit(solution)/shard_map/ppermute | solution.py:251
  22.6 5.7 %collective-permute-done.5.d1 = bf16[512,256]{1,0:T(8,128)(2,1)S(1)} collective-permute-done((bf16[512,256]{1,0:T(8,128)(2,1)}, bf16[512,256]{1,0:T(8,128)(2,1)S(1)}, u32[]{:S(2)}, u32[]{:S(2)}) %collective-permute-start.5) | collective-permute-done | bytes 262176 | tf_op jit(solution)/shard_map/ppermute | solution.py:251
  28.3 5.1 %collective-permute-done.6.d2 = bf16[512,256]{1,0:T(8,128)(2,1)S(1)} collective-permute-done((bf16[512,256]{1,0:T(8,128)(2,1)}, bf16[512,256]{1,0:T(8,128)(2,1)S(1)}, u32[]{:S(2)}, u32[]{:S(2)}) %collective-permute-start.6) | collective-permute-done | bytes 262176 | tf_op jit(solution)/shard_map/ppermute | solution.py:251
  37.2 5.3 %collective-permute-done.8.d1 = bf16[512,256]{1,0:T(8,128)(2,1)S(1)} collective-permute-done((bf16[512,256]{1,0:T(8,128)(2,1)S(1)}, bf16[512,256]{1,0:T(8,128)(2,1)S(1)}, u32[]{:S(2)}, u32[]{:S(2)}) %collective-permute-start.8) | collective-permute-done | bytes 262176 | tf_op jit(solution)/shard_map/ppermute | solution.py:251
  42.5 3.2 %collective-permute-done.9.d2 = bf16[512,256]{1,0:T(8,128)(2,1)S(1)} collective-permute-done((bf16[512,256]{1,0:T(8,128)(2,1)S(1)}, bf16[512,256]{1,0:T(8,128)(2,1)S(1)}, u32[]{:S(2)}, u32[]{:S(2)}) %collective-permute-start.9) | collective-permute-done | bytes 262176 | tf_op jit(solution)/shard_map/ppermute | solution.py:251
  50.0 2.8 %copy-done = bf16[48,256,256]{2,1,0:T(8,128)(2,1)S(1)} copy-done((bf16[48,256,256]{2,1,0:T(8,128)(2,1)S(1)}, bf16[48,256,256]{2,1,0:T(8,128)(2,1)}, u32[]{:S(2)}) %copy-start) | copy-done | bytes 6291480
  52.8 7.7 %products.3 = (s16[8,272,256]{2,1,0:T(8,128)(2,1)}, f32[8,256,256]{2,1,0:T(8,128)S(1)}) custom-call(s32[3]{0:T(128)S(1)} %pad_add_fusion.2.ends_ref, s32[2,48]{1,0:T(2,128)S(1)} %get-tuple-element.71.source_ref, s32[2,48]{1,0:T(2,128)S(1)} %get-tuple-element.86.slot_ref, s32[2,48]{1,0:T(2,128)S(1)} %get-tuple-element.69.label_ref, ...), custom_call_target="tpu_custom_call" | custom-call | flops 1610612736 | bytes 12582912 | tf_op jit(solution)/shard_map/products/pallas_call | solution.py:310
  61.7 6.3 %products.4 = (s16[8,272,256]{2,1,0:T(8,128)(2,1)S(1)}, f32[8,256,256]{2,1,0:T(8,128)S(1)}) custom-call(s32[3]{0:T(128)S(1)} %pad_add_fusion.2.ends_ref, s32[2,48]{1,0:T(2,128)S(1)} %get-tuple-element.71.source_ref, s32[2,48]{1,0:T(2,128)S(1)} %get-tuple-element.85.slot_ref, s32[2,48]{1,0:T(2,128)S(1)} %get-tuple-element.69.label_ref, ...), custom_call_target="tpu_custom_call" | custom-call | flops 1610612736 | bytes 12582912 | tf_op jit(solution)/shard_map/products/pallas_call | solution.py:310
  70.1 6.3 %products.5 = (s16[8,272,256]{2,1,0:T(8,128)(2,1)S(1)}, f32[8,256,256]{2,1,0:T(8,128)S(1)}) custom-call(s32[3]{0:T(128)S(1)} %pad_add_fusion.2.ends_ref, s32[2,48]{1,0:T(2,128)S(1)} %get-tuple-element.71.source_ref, s32[2,48]{1,0:T(2,128)S(1)} %get-tuple-element.84.slot_ref, s32[2,48]{1,0:T(2,128)S(1)} %get-tuple-element.69.label_ref, ...), custom_call_target="tpu_custom_call" | custom-call | flops 1610612736 | bytes 12582912 | tf_op jit(solution)/shard_map/products/pallas_call | solution.py:310
  78.0 9.5 %collective-permute-done.14.recv = s16[8,272,256]{2,1,0:T(8,128)(2,1)S(1)} collective-permute-done((s16[8,272,256]{2,1,0:T(8,128)(2,1)}, s16[8,272,256]{2,1,0:T(8,128)(2,1)S(1)}, u32[]{:S(2)}, u32[]{:S(2)}) %collective-permute-start.14) | collective-permute-done | bytes 1114144 | tf_op jit(solution)/shard_map/ppermute | solution.py:262
  90.1 2.9 %collective-permute-done.21.recv = s16[8,272,256]{2,1,0:T(8,128)(2,1)S(1)} collective-permute-done((s16[8,272,256]{2,1,0:T(8,128)(2,1)S(1)}, s16[8,272,256]{2,1,0:T(8,128)(2,1)S(1)}, u32[]{:S(2)}, u32[]{:S(2)}) %collective-permute-start.21) | collective-permute-done | bytes 1114144 | tf_op jit(solution)/shard_map/ppermute | solution.py:251
  93.6 4.6 %collective-permute-start.22 = (s16[4,272,256]{2,1,0:T(8,128)(2,1)S(1)}, s16[4,272,256]{2,1,0:T(8,128)(2,1)S(1)}, u32[]{:S(2)}, u32[]{:S(2)}) collective-permute-start(s16[4,272,256]{2,1,0:T(8,128)(2,1)S(1)} %get-tuple-element.52), channel_id=1, source_target_pairs={{0,8},{8,0},{16,24},{24,16},{1,9},{9,1},{17,25},{25,17},{2,10},{10... | collective-permute-start | bytes 1671176 | tf_op jit(solution)/shard_map/ppermute | solution.py:251
  101.4 3.2 %collective-permute-start.29 = (s16[4,272,256]{2,1,0:T(8,128)(2,1)S(1)}, s16[4,272,256]{2,1,0:T(8,128)(2,1)S(1)}, u32[]{:S(2)}, u32[]{:S(2)}) collective-permute-start(s16[4,272,256]{2,1,0:T(8,128)(2,1)S(1)} %get-tuple-element.63), channel_id=1, source_target_pairs={{0,16},{8,24},{16,0},{24,8},{1,17},{9,25},{17,1},{25,9},{2,18},{10... | collective-permute-start | bytes 1671176 | tf_op jit(solution)/shard_map/ppermute | solution.py:251
  105.3 4.6 %collective-permute-start.16 = (s16[2,272,256]{2,1,0:T(8,128)(2,1)S(1)}, s16[2,272,256]{2,1,0:T(8,128)(2,1)S(1)}, u32[]{:S(2)}, u32[]{:S(2)}) collective-permute-start(s16[2,272,256]{2,1,0:T(8,128)(2,1)S(1)} %get-tuple-element.43), channel_id=1, source_target_pairs={{0,8},{8,0},{16,24},{24,16},{1,9},{9,1},{17,25},{25,17},{2,10},{10... | collective-permute-start | bytes 835592 | tf_op jit(solution)/shard_map/ppermute | solution.py:251
  109.9 2.8 %collective-permute-done.22.recv = s16[4,272,256]{2,1,0:T(8,128)(2,1)S(1)} collective-permute-done((s16[4,272,256]{2,1,0:T(8,128)(2,1)S(1)}, s16[4,272,256]{2,1,0:T(8,128)(2,1)S(1)}, u32[]{:S(2)}, u32[]{:S(2)}) %collective-permute-start.22) | collective-permute-done | bytes 557088 | tf_op jit(solution)/shard_map/ppermute | solution.py:251
  113.6 3.8 %collective-permute-done.29.recv = s16[4,272,256]{2,1,0:T(8,128)(2,1)S(1)} collective-permute-done((s16[4,272,256]{2,1,0:T(8,128)(2,1)S(1)}, s16[4,272,256]{2,1,0:T(8,128)(2,1)S(1)}, u32[]{:S(2)}, u32[]{:S(2)}) %collective-permute-start.29) | collective-permute-done | bytes 557088 | tf_op jit(solution)/shard_map/ppermute | solution.py:251
  119.4 4.3 %collective-permute-start.17 = (s16[1,272,256]{2,1,0:T(8,128)(2,1)S(1)}, s16[1,272,256]{2,1,0:T(8,128)(2,1)S(1)}, u32[]{:S(2)}, u32[]{:S(2)}) collective-permute-start(s16[1,272,256]{2,1,0:T(8,128)(2,1)S(1)} %get-tuple-element.45), channel_id=1, source_target_pairs={{0,4},{1,5},{2,6},{3,7},{4,0},{5,1},{6,2},{7,3},{8,12},{9,13},{10,... | collective-permute-start | bytes 417800 | tf_op jit(solution)/shard_map/ppermute | solution.py:262
  124.8 6.5 %collective-permute-done.30.recv = s16[2,272,256]{2,1,0:T(8,128)(2,1)S(1)} collective-permute-done((s16[2,272,256]{2,1,0:T(8,128)(2,1)S(1)}, s16[2,272,256]{2,1,0:T(8,128)(2,1)S(1)}, u32[]{:S(2)}, u32[]{:S(2)}) %collective-permute-start.30) | collective-permute-done | bytes 278560 | tf_op jit(solution)/shard_map/ppermute | solution.py:262
  131.4 3.6 %collective-permute-start.31 = (s16[1,272,256]{2,1,0:T(8,128)(2,1)S(1)}, s16[1,272,256]{2,1,0:T(8,128)(2,1)S(1)}, u32[]{:S(2)}, u32[]{:S(2)}) collective-permute-start(s16[1,272,256]{2,1,0:T(8,128)(2,1)S(1)} %get-tuple-element.67), channel_id=1, source_target_pairs={{0,4},{1,5},{2,6},{3,7},{4,0},{5,1},{6,2},{7,3},{8,12},{9,13},{10,... | collective-permute-start | bytes 417800 | tf_op jit(solution)/shard_map/ppermute | solution.py:262
  135.1 11.3 %all-gather = s16[1088,256]{1,0:T(8,128)(2,1)S(1)} all-gather(s16[272,256]{1,0:T(8,128)(2,1)S(1)} %finish.3), channel_id=2, replica_groups=mesh['grp'=4,'wide'=8] {'grp'}, dimensions={0}, use_global_device_ids=true | all-gather | bytes 696320 | tf_op jit(solution)/shard_map/all_gather | solution.py:364
  146.5 11.3 %all-gather.1 = s16[1088,256]{1,0:T(8,128)(2,1)S(1)} all-gather(s16[272,256]{1,0:T(8,128)(2,1)S(1)} %finish.4), channel_id=3, replica_groups=mesh['grp'=4,'wide'=8] {'grp'}, dimensions={0}, use_global_device_ids=true | all-gather | bytes 696320 | tf_op jit(solution)/shard_map/all_gather | solution.py:364
  157.9 9.4 %all-gather.2 = s16[1088,256]{1,0:T(8,128)(2,1)S(1)} all-gather(s16[272,256]{1,0:T(8,128)(2,1)S(1)} %finish.5), channel_id=4, replica_groups=mesh['grp'=4,'wide'=8] {'grp'}, dimensions={0}, use_global_device_ids=true | all-gather | bytes 696320 | tf_op jit(solution)/shard_map/all_gather | solution.py:364
  (81 shorter events, 37.6 us)
Async XLA Ops:
  0.0 49.9 %collective-permute-start.1 = (bf16[48,256,256]{2,1,0:T(8,128)(2,1)}, bf16[48,256,256]{2,1,0:T(8,128)(2,1)}, u32[]{:S(2)}, u32[]{:S(2)}) collective-permute-start(bf16[48,256,256]{2,1,0:T(8,128)(2,1)} %own_tiles.5), channel_id=1, source_target_pairs={{0,1},{1,0},{2,3},{3,2},{4,5},{5,4},{6,7},{7,6},{8,9},{9,8},{10,11... | collective-permute-start | bytes 18874376 | tf_op jit(solution)/shard_map/ppermute | solution.py:248
  5.0 13.9 %collective-permute-start.3 = (bf16[512,256]{1,0:T(8,128)(2,1)S(1)}, bf16[512,256]{1,0:T(8,128)(2,1)S(1)}, u32[]{:S(2)}, u32[]{:S(2)}) collective-permute-start(bf16[512,256]{1,0:T(8,128)(2,1)S(1)} %get-tuple-element.79), channel_id=1, source_target_pairs={{0,16},{8,24},{16,0},{24,8},{1,17},{9,25},{17,1},{25,9},{2,18},{10... | collective-permute-start | bytes 786440 | tf_op jit(solution)/shard_map/ppermute | solution.py:251
  6.5 12.4 %collective-permute-start.4 = (bf16[512,256]{1,0:T(8,128)(2,1)S(1)}, bf16[512,256]{1,0:T(8,128)(2,1)S(1)}, u32[]{:S(2)}, u32[]{:S(2)}) collective-permute-start(bf16[512,256]{1,0:T(8,128)(2,1)S(1)} %get-tuple-element.79), channel_id=1, source_target_pairs={{0,24},{8,16},{16,8},{24,0},{1,25},{9,17},{17,9},{25,1},{2,26},{10... | collective-permute-start | bytes 786440 | tf_op jit(solution)/shard_map/ppermute | solution.py:251
  20.1 13.3 %collective-permute-start.6 = (bf16[512,256]{1,0:T(8,128)(2,1)}, bf16[512,256]{1,0:T(8,128)(2,1)S(1)}, u32[]{:S(2)}, u32[]{:S(2)}) collective-permute-start(bf16[512,256]{1,0:T(8,128)(2,1)} %get-tuple-element.37), channel_id=1, source_target_pairs={{0,16},{8,24},{16,0},{24,8},{1,17},{9,25},{17,1},{25,9},{2,18},{10... | collective-permute-start | bytes 786440 | tf_op jit(solution)/shard_map/ppermute | solution.py:251
  20.9 12.5 %collective-permute-start.7 = (bf16[512,256]{1,0:T(8,128)(2,1)}, bf16[512,256]{1,0:T(8,128)(2,1)S(1)}, u32[]{:S(2)}, u32[]{:S(2)}) collective-permute-start(bf16[512,256]{1,0:T(8,128)(2,1)} %get-tuple-element.37), channel_id=1, source_target_pairs={{0,24},{8,16},{16,8},{24,0},{1,25},{9,17},{17,9},{25,1},{2,26},{10... | collective-permute-start | bytes 786440 | tf_op jit(solution)/shard_map/ppermute | solution.py:251
  34.0 11.7 %collective-permute-start.9 = (bf16[512,256]{1,0:T(8,128)(2,1)S(1)}, bf16[512,256]{1,0:T(8,128)(2,1)S(1)}, u32[]{:S(2)}, u32[]{:S(2)}) collective-permute-start(bf16[512,256]{1,0:T(8,128)(2,1)S(1)} %get-tuple-element.38), channel_id=1, source_target_pairs={{0,16},{8,24},{16,0},{24,8},{1,17},{9,25},{17,1},{25,9},{2,18},{10... | collective-permute-start | bytes 786440 | tf_op jit(solution)/shard_map/ppermute | solution.py:251
  35.4 10.3 %collective-permute-start.10 = (bf16[512,256]{1,0:T(8,128)(2,1)S(1)}, bf16[512,256]{1,0:T(8,128)(2,1)S(1)}, u32[]{:S(2)}, u32[]{:S(2)}) collective-permute-start(bf16[512,256]{1,0:T(8,128)(2,1)S(1)} %get-tuple-element.38), channel_id=1, source_target_pairs={{0,24},{8,16},{16,8},{24,0},{1,25},{9,17},{17,9},{25,1},{2,26},{10... | collective-permute-start | bytes 786440 | tf_op jit(solution)/shard_map/ppermute | solution.py:251
  46.9 13.6 %collective-permute-start.19 = (bf16[512,256]{1,0:T(8,128)(2,1)S(1)}, bf16[512,256]{1,0:T(8,128)(2,1)S(1)}, u32[]{:S(2)}, u32[]{:S(2)}) collective-permute-start(bf16[512,256]{1,0:T(8,128)(2,1)S(1)} %collective-permute-done.6.d2), channel_id=1, source_target_pairs={{0,1},{1,0},{2,3},{3,2},{4,5},{5,4},{6,7},{7,6},{8,9},{9,8},{10,11... | collective-permute-start | bytes 786440 | tf_op jit(solution)/shard_map/ppermute | solution.py:248
  47.0 14.7 %collective-permute-start.20 = (bf16[512,256]{1,0:T(8,128)(2,1)S(1)}, bf16[512,256]{1,0:T(8,128)(2,1)S(1)}, u32[]{:S(2)}, u32[]{:S(2)}) collective-permute-start(bf16[512,256]{1,0:T(8,128)(2,1)S(1)} %collective-permute-done.7.d3), channel_id=1, source_target_pairs={{0,1},{1,0},{2,3},{3,2},{4,5},{5,4},{6,7},{7,6},{8,9},{9,8},{10,11... | collective-permute-start | bytes 786440 | tf_op jit(solution)/shard_map/ppermute | solution.py:248
  49.4 20.7 %collective-permute-start.25 = (bf16[512,256]{1,0:T(8,128)(2,1)S(1)}, bf16[512,256]{1,0:T(8,128)(2,1)S(1)}, u32[]{:S(2)}, u32[]{:S(2)}) collective-permute-start(bf16[512,256]{1,0:T(8,128)(2,1)S(1)} %collective-permute-done.2.d1), channel_id=1, source_target_pairs={{0,1},{1,0},{2,3},{3,2},{4,5},{5,4},{6,7},{7,6},{8,9},{9,8},{10,11... | collective-permute-start | bytes 786440 | tf_op jit(solution)/shard_map/ppermute | solution.py:248
  49.5 20.6 %collective-permute-start.26 = (bf16[512,256]{1,0:T(8,128)(2,1)S(1)}, bf16[512,256]{1,0:T(8,128)(2,1)S(1)}, u32[]{:S(2)}, u32[]{:S(2)}) collective-permute-start(bf16[512,256]{1,0:T(8,128)(2,1)S(1)} %collective-permute-done.3.d2), channel_id=1, source_target_pairs={{0,1},{1,0},{2,3},{3,2},{4,5},{5,4},{6,7},{7,6},{8,9},{9,8},{10,11... | collective-permute-start | bytes 786440 | tf_op jit(solution)/shard_map/ppermute | solution.py:248
  49.9 20.1 %collective-permute-start.27 = (bf16[512,256]{1,0:T(8,128)(2,1)S(1)}, bf16[512,256]{1,0:T(8,128)(2,1)S(1)}, u32[]{:S(2)}, u32[]{:S(2)}) collective-permute-start(bf16[512,256]{1,0:T(8,128)(2,1)S(1)} %collective-permute-done.4.d3), channel_id=1, source_target_pairs={{0,1},{1,0},{2,3},{3,2},{4,5},{5,4},{6,7},{7,6},{8,9},{9,8},{10,11... | collective-permute-start | bytes 786440 | tf_op jit(solution)/shard_map/ppermute | solution.py:248
  60.5 27.0 %collective-permute-start.14 = (s16[8,272,256]{2,1,0:T(8,128)(2,1)}, s16[8,272,256]{2,1,0:T(8,128)(2,1)S(1)}, u32[]{:S(2)}, u32[]{:S(2)}) collective-permute-start(s16[8,272,256]{2,1,0:T(8,128)(2,1)} %get-tuple-element.39), channel_id=1, source_target_pairs={{0,2},{1,3},{2,0},{3,1},{4,6},{5,7},{6,4},{7,5},{8,10},{9,11},{10,... | collective-permute-start | bytes 3342344 | tf_op jit(solution)/shard_map/ppermute | solution.py:262
  68.0 25.0 %collective-permute-start.21 = (s16[8,272,256]{2,1,0:T(8,128)(2,1)S(1)}, s16[8,272,256]{2,1,0:T(8,128)(2,1)S(1)}, u32[]{:S(2)}, u32[]{:S(2)}) collective-permute-start(s16[8,272,256]{2,1,0:T(8,128)(2,1)S(1)} %get-tuple-element.50), channel_id=1, source_target_pairs={{0,16},{8,24},{16,0},{24,8},{1,17},{9,25},{17,1},{25,9},{2,18},{10... | collective-permute-start | bytes 3342344 | tf_op jit(solution)/shard_map/ppermute | solution.py:251
  76.4 24.4 %collective-permute-start.28 = (s16[8,272,256]{2,1,0:T(8,128)(2,1)S(1)}, s16[8,272,256]{2,1,0:T(8,128)(2,1)S(1)}, u32[]{:S(2)}, u32[]{:S(2)}) collective-permute-start(s16[8,272,256]{2,1,0:T(8,128)(2,1)S(1)} %get-tuple-element.61), channel_id=1, source_target_pairs={{0,8},{8,0},{16,24},{24,16},{1,9},{9,1},{17,25},{25,17},{2,10},{10... | collective-permute-start | bytes 3342344 | tf_op jit(solution)/shard_map/ppermute | solution.py:251
  88.2 16.8 %collective-permute-start.15 = (s16[4,272,256]{2,1,0:T(8,128)(2,1)S(1)}, s16[4,272,256]{2,1,0:T(8,128)(2,1)S(1)}, u32[]{:S(2)}, u32[]{:S(2)}) collective-permute-start(s16[4,272,256]{2,1,0:T(8,128)(2,1)S(1)} %get-tuple-element.41), channel_id=1, source_target_pairs={{0,16},{8,24},{16,0},{24,8},{1,17},{9,25},{17,1},{25,9},{2,18},{10... | collective-permute-start | bytes 1671176 | tf_op jit(solution)/shard_map/ppermute | solution.py:251
  93.6 19.1 %collective-permute-start.22 = (s16[4,272,256]{2,1,0:T(8,128)(2,1)S(1)}, s16[4,272,256]{2,1,0:T(8,128)(2,1)S(1)}, u32[]{:S(2)}, u32[]{:S(2)}) collective-permute-start(s16[4,272,256]{2,1,0:T(8,128)(2,1)S(1)} %get-tuple-element.52), channel_id=1, source_target_pairs={{0,8},{8,0},{16,24},{24,16},{1,9},{9,1},{17,25},{25,17},{2,10},{10... | collective-permute-start | bytes 1671176 | tf_op jit(solution)/shard_map/ppermute | solution.py:251
  101.4 16.0 %collective-permute-start.29 = (s16[4,272,256]{2,1,0:T(8,128)(2,1)S(1)}, s16[4,272,256]{2,1,0:T(8,128)(2,1)S(1)}, u32[]{:S(2)}, u32[]{:S(2)}) collective-permute-start(s16[4,272,256]{2,1,0:T(8,128)(2,1)S(1)} %get-tuple-element.63), channel_id=1, source_target_pairs={{0,16},{8,24},{16,0},{24,8},{1,17},{9,25},{17,1},{25,9},{2,18},{10... | collective-permute-start | bytes 1671176 | tf_op jit(solution)/shard_map/ppermute | solution.py:251
  105.3 14.0 %collective-permute-start.16 = (s16[2,272,256]{2,1,0:T(8,128)(2,1)S(1)}, s16[2,272,256]{2,1,0:T(8,128)(2,1)S(1)}, u32[]{:S(2)}, u32[]{:S(2)}) collective-permute-start(s16[2,272,256]{2,1,0:T(8,128)(2,1)S(1)} %get-tuple-element.43), channel_id=1, source_target_pairs={{0,8},{8,0},{16,24},{24,16},{1,9},{9,1},{17,25},{25,17},{2,10},{10... | collective-permute-start | bytes 835592 | tf_op jit(solution)/shard_map/ppermute | solution.py:251
  113.0 10.7 %collective-permute-start.23 = (s16[2,272,256]{2,1,0:T(8,128)(2,1)S(1)}, s16[2,272,256]{2,1,0:T(8,128)(2,1)S(1)}, u32[]{:S(2)}, u32[]{:S(2)}) collective-permute-start(s16[2,272,256]{2,1,0:T(8,128)(2,1)S(1)} %get-tuple-element.54), channel_id=1, source_target_pairs={{0,2},{1,3},{2,0},{3,1},{4,6},{5,7},{6,4},{7,5},{8,10},{9,11},{10,... | collective-permute-start | bytes 835592 | tf_op jit(solution)/shard_map/ppermute | solution.py:262
  117.7 13.6 %collective-permute-start.30 = (s16[2,272,256]{2,1,0:T(8,128)(2,1)S(1)}, s16[2,272,256]{2,1,0:T(8,128)(2,1)S(1)}, u32[]{:S(2)}, u32[]{:S(2)}) collective-permute-start(s16[2,272,256]{2,1,0:T(8,128)(2,1)S(1)} %get-tuple-element.65), channel_id=1, source_target_pairs={{0,2},{1,3},{2,0},{3,1},{4,6},{5,7},{6,4},{7,5},{8,10},{9,11},{10,... | collective-permute-start | bytes 835592 | tf_op jit(solution)/shard_map/ppermute | solution.py:262
  119.4 15.6 %collective-permute-start.17 = (s16[1,272,256]{2,1,0:T(8,128)(2,1)S(1)}, s16[1,272,256]{2,1,0:T(8,128)(2,1)S(1)}, u32[]{:S(2)}, u32[]{:S(2)}) collective-permute-start(s16[1,272,256]{2,1,0:T(8,128)(2,1)S(1)} %get-tuple-element.45), channel_id=1, source_target_pairs={{0,4},{1,5},{2,6},{3,7},{4,0},{5,1},{6,2},{7,3},{8,12},{9,13},{10,... | collective-permute-start | bytes 417800 | tf_op jit(solution)/shard_map/ppermute | solution.py:262
  123.9 22.5 %collective-permute-start.24 = (s16[1,272,256]{2,1,0:T(8,128)(2,1)S(1)}, s16[1,272,256]{2,1,0:T(8,128)(2,1)S(1)}, u32[]{:S(2)}, u32[]{:S(2)}) collective-permute-start(s16[1,272,256]{2,1,0:T(8,128)(2,1)S(1)} %get-tuple-element.56), channel_id=1, source_target_pairs={{0,4},{1,5},{2,6},{3,7},{4,0},{5,1},{6,2},{7,3},{8,12},{9,13},{10,... | collective-permute-start | bytes 417800 | tf_op jit(solution)/shard_map/ppermute | solution.py:262
  131.4 26.4 %collective-permute-start.31 = (s16[1,272,256]{2,1,0:T(8,128)(2,1)S(1)}, s16[1,272,256]{2,1,0:T(8,128)(2,1)S(1)}, u32[]{:S(2)}, u32[]{:S(2)}) collective-permute-start(s16[1,272,256]{2,1,0:T(8,128)(2,1)S(1)} %get-tuple-element.67), channel_id=1, source_target_pairs={{0,4},{1,5},{2,6},{3,7},{4,0},{5,1},{6,2},{7,3},{8,12},{9,13},{10,... | collective-permute-start | bytes 417800 | tf_op jit(solution)/shard_map/ppermute | solution.py:262
  (11 other events, 114.7 us)
